TPU v7x, 32 devices: a whole 2x2x4 slice. The times are simulated.
32 devices in a mesh: dp: 4 (over x, core), group: 8 (over z, y).
Axes of the slice: x: 2, y: 2, z: 4, core: 2. Of those that a mesh axis runs over, the one named last changes fastest.
Arguments:
- embeds: bfloat16 [8192, 1024], P(('dp', 'group')), may hold values from -6 to 6
- row_ids: int32 [8192], P(('dp', 'group')), may hold values from 0 to 63
- neighbors: int32 [32, 3], P('dp'), may hold values from 0 to 7, as said below
- w_first: bfloat16 [1024, 4096], P(None, 'dp'), may hold values from -0.1875 to 0.1875
- w_second: bfloat16 [4096, 1024], P('dp'), may hold values from -0.09375 to 0.09375
Outputs:
- grad_first: float32 [1024, 4096], P('group', 'dp')
- grad_second: float32 [4096, 1024], P('dp', 'group')
- grad_unit: float32 [8192, 1024], P(('dp', 'group'))
Inputs may be any that keep to these rules, and one draw needn't show every extreme that they name: `neighbors`: within a row the 3 entries differ from one another and from the row's own index b % 8.
All inputs are finite; a program needn't handle non-finite values.
Results may differ from a plain program's by a relative error of at most 0.013.
Values may be sent and summed in bfloat16 or wider, within the bound.
A program may use at most 64 MiB of HBM per device.

v0:
```python
import functools

import jax
import jax.numpy as jnp
from jax import lax
from jax.experimental import pallas as pl
from jax.experimental.pallas import tpu as pltpu
from jax.sharding import PartitionSpec as P

EPS = 1e-06
TEMP = 10.0
SHIFT = -5.0
LEVELS = 32000.0
LANES = 128
CHUNK = 256
UNIT_PARTS = 4
VMEM_BYTES = 60 * 1024 * 1024
MESH = pl.DeviceIdType.MESH


def gelu_fwd(value):
    return jax.nn.gelu(value, approximate=True)


def gelu_back(pre, grad):
    _, back = jax.vjp(gelu_fwd, pre)
    return back(grad)[0]


def encode(value):
    flat = value.reshape(-1, value.shape[-1])
    top = jnp.max(jnp.abs(flat), axis=0, keepdims=True)
    joint = top[:, :LANES]
    for at in range(LANES, top.shape[1], LANES):
        joint = jnp.maximum(joint, top[:, at : at + LANES])
    joint = jnp.maximum(joint, 1e-30)
    inverse = jnp.tile(LEVELS / joint, (1, top.shape[1] // LANES))
    code = jnp.round(flat * inverse).astype(jnp.int32).astype(jnp.int16)
    return code.reshape(value.shape), jnp.broadcast_to(joint * (1.0 / LEVELS), (8, LANES))


def decode(code, scale):
    wide = jnp.tile(scale[0:1], (1, code.shape[-1] // LANES))
    return code.astype(jnp.int32).astype(jnp.float32) * wide


def weight_kernel(
    n_y,
    n_z,
    left0,
    left1,
    hidden,
    pre,
    grads,
    w_second,
    out,
    grad_pre,
    own,
    mine,
    y_out,
    y_in,
    y_scale_out,
    y_scale_in,
    z_out,
    z_in,
    z_scale_out,
    z_scale_in,
    y_sems,
    z_sems,
):
    me = lax.axis_index("group")
    z, y = me // n_y, me % n_y
    tall = out.shape[1]
    chunks = out.shape[2] // CHUNK

    def y_peer(d):
        return z * n_y + lax.rem(y + d, n_y)

    def z_peer(d):
        return lax.rem(z + d, n_z) * n_y + y

    def y_copies(i, d):
        return [
            pltpu.make_async_remote_copy(
                src_ref=a.at[i, d - 1],
                dst_ref=b.at[i, d - 1],
                send_sem=y_sems.at[which, 0, i, d - 1],
                recv_sem=y_sems.at[which, 1, i, d - 1],
                device_id={"group": y_peer(d)},
                device_id_type=MESH,
            )
            for which, (a, b) in enumerate(((y_out, y_in), (y_scale_out, y_scale_in)))
        ]

    def z_copies(i, d):
        return [
            pltpu.make_async_remote_copy(
                src_ref=a.at[i, d - 1],
                dst_ref=b.at[i, d - 1],
                send_sem=z_sems.at[which, 0, i, d - 1],
                recv_sem=z_sems.at[which, 1, i, d - 1],
                device_id={"group": z_peer(d)},
                device_id_type=MESH,
            )
            for which, (a, b) in enumerate(((z_out, z_in), (z_scale_out, z_scale_in)))
        ]

    barrier = pltpu.get_barrier_semaphore()
    for d in range(1, n_y):
        pl.semaphore_signal(barrier, inc=1, device_id={"group": y_peer(d)}, device_id_type=MESH)
    for d in range(1, n_z):
        pl.semaphore_signal(barrier, inc=1, device_id={"group": z_peer(d)}, device_id_type=MESH)
    pl.semaphore_wait(barrier, n_y + n_z - 2)

    def send_partials(i, left, rhs):
        def partial(owner_y, row):
            at = pl.multiple_of((row * n_y + owner_y) * tall, tall)
            return jnp.dot(left[pl.ds(at, tall), :], rhs, preferred_element_type=jnp.float32)

        for d in range(1, n_y):
            blocks = jnp.stack([partial(lax.rem(y + d, n_y), row) for row in range(n_z)])
            code, scale = encode(blocks)
            y_out[i, d - 1] = code
            y_scale_out[i, d - 1] = scale
            for copy in y_copies(i, d):
                copy.start()
        for row in range(n_z):
            own[i, row] = partial(y, row)

    def send_sums(i):
        for d in range(1, n_y):
            for copy in y_copies(i, d):
                copy.wait_recv()
        for d in range(1, n_z):
            row = lax.rem(z + d, n_z)
            block = own[i, row]
            for e in range(1, n_y):
                block = block + decode(y_in[i, e - 1, row], y_scale_in[i, e - 1])
            code, scale = encode(block)
            z_out[i, d - 1] = code
            z_scale_out[i, d - 1] = scale
            for copy in z_copies(i, d):
                copy.start()
        block = own[i, z]
        for e in range(1, n_y):
            block = block + decode(y_in[i, e - 1, z], y_scale_in[i, e - 1])
        mine[i] = block

    @pl.loop(0, chunks)
    def _(k):
        columns = pl.ds(pl.multiple_of(k * CHUNK, CHUNK), CHUNK)
        send_partials(k, left0, hidden[:, columns])

    @pl.loop(0, chunks)
    def _(k):
        columns = pl.ds(pl.multiple_of(k * CHUNK, CHUNK), CHUNK)
        w_rows = w_second[columns, :]

        @pl.loop(0, pre.shape[0] // CHUNK)
        def _(r):
            rows = pl.ds(pl.multiple_of(r * CHUNK, CHUNK), CHUNK)
            grad_hidden = lax.dot_general(
                grads[rows, :], w_rows, (((1,), (1,)), ((), ())), preferred_element_type=jnp.float32
            )
            grad_pre[rows, :] = gelu_back(pre[rows, columns], grad_hidden).astype(jnp.bfloat16)

        send_partials(chunks + k, left1, grad_pre[...])
        send_sums(k)

    @pl.loop(chunks, 2 * chunks)
    def _(i):
        send_sums(i)

    for m in range(2):

        @pl.loop(0, chunks)
        def _(k, m=m):
            i = m * chunks + k
            block = mine[i]
            for d in range(1, n_z):
                for copy in z_copies(i, d):
                    copy.wait_recv()
            for d in range(1, n_z):
                block = block + decode(z_in[i, d - 1], z_scale_in[i, d - 1])
            out[m, :, pl.ds(pl.multiple_of(k * CHUNK, CHUNK), CHUNK)] = block

    @pl.loop(0, 2 * chunks)
    def _(i):
        for d in range(1, n_y):
            for copy in y_copies(i, d):
                copy.wait_send()
        for d in range(1, n_z):
            for copy in z_copies(i, d):
                copy.wait_send()


def split(owners, shares):
    return shares // 2 if owners % (shares // 2) == 0 else 1


def weight_sums(left0, left1, hidden, pre, grads, w_second):
    owners, shares = lax.axis_size("group"), lax.axis_size("dp")
    n_y = split(owners, shares)
    n_z = owners // n_y
    tall = left0.shape[0] // owners
    wide = hidden.shape[1]
    items = 2 * (wide // CHUNK)
    vmem = pl.BlockSpec(memory_space=pltpu.VMEM)
    return pl.pallas_call(
        functools.partial(weight_kernel, n_y, n_z),
        out_shape=jax.ShapeDtypeStruct((2, tall, wide), jnp.float32),
        in_specs=[vmem] * 6,
        out_specs=vmem,
        scratch_shapes=[
            pltpu.VMEM((hidden.shape[0], CHUNK), jnp.bfloat16),
            pltpu.VMEM((items, n_z, tall, CHUNK), jnp.float32),
            pltpu.VMEM((items, tall, CHUNK), jnp.float32),
            pltpu.VMEM((items, n_y - 1, n_z, tall, CHUNK), jnp.int16),
            pltpu.VMEM((items, n_y - 1, n_z, tall, CHUNK), jnp.int16),
            pltpu.VMEM((items, n_y - 1, 8, LANES), jnp.float32),
            pltpu.VMEM((items, n_y - 1, 8, LANES), jnp.float32),
            pltpu.VMEM((items, n_z - 1, tall, CHUNK), jnp.int16),
            pltpu.VMEM((items, n_z - 1, tall, CHUNK), jnp.int16),
            pltpu.VMEM((items, n_z - 1, 8, LANES), jnp.float32),
            pltpu.VMEM((items, n_z - 1, 8, LANES), jnp.float32),
            pltpu.SemaphoreType.DMA((2, 2, items, n_y - 1)),
            pltpu.SemaphoreType.DMA((2, 2, items, n_z - 1)),
        ],
        compiler_params=pltpu.CompilerParams(
            collective_id=0, has_side_effects=True, vmem_limit_bytes=VMEM_BYTES
        ),
    )(left0, left1, hidden, pre, grads, w_second)


def front_kernel(
    n_x,
    n_y,
    n_z,
    embeds,
    ids_col,
    ids_row,
    times,
    w_first,
    w_second,
    gathered_t,
    pre,
    hidden,
    grad_unit,
    grads,
    grads_t,
    gathered,
    ids,
    units,
    unit,
    inverse,
    grad_all,
    core_out,
    core_in,
    x_out,
    x_in,
    kept,
    id_sems,
    gx_sems,
    gc_sems,
    pc_sems,
    px_sems,
    uz_sems,
    uy_sems,
):
    share, me = lax.axis_index("dp"), lax.axis_index("group")
    x, core = share // 2, share % 2
    z, y = me // n_y, me % n_y
    block, width = embeds.shape
    half = block // 2
    part = block // UNIT_PARTS
    n_g = n_y * n_z

    def remote(src, dst, sems, at, device):
        return pltpu.make_async_remote_copy(
            src_ref=src,
            dst_ref=dst,
            send_sem=sems.at[(0,) + at],
            recv_sem=sems.at[(1,) + at],
            device_id=device,
            device_id_type=MESH,
        )

    def share_at(dx, other):
        return lax.rem(x + n_x - dx, n_x) * 2 + (1 - core if other else core)

    def x_peer(d):
        return {"dp": lax.rem(x + d, n_x) * 2 + core}

    core_peer = {"dp": x * 2 + 1 - core}

    def owner_at(dz, dy):
        return lax.rem(z + n_z - dz, n_z) * n_y + lax.rem(y + n_y - dy, n_y)

    def z_peer(d):
        return {"group": lax.rem(z + d, n_z) * n_y + y}

    def y_peer(d):
        return {"group": z * n_y + lax.rem(y + d, n_y)}

    def g_peer(d):
        return {"group": lax.rem(me + d, n_g)}

    def rows(at, count):
        return pl.ds(pl.multiple_of(at, count), count)

    barrier = pltpu.get_barrier_semaphore()
    for d in range(1, n_x):
        pl.semaphore_signal(barrier, inc=1, device_id=x_peer(d), device_id_type=MESH)
    pl.semaphore_signal(barrier, inc=1, device_id=core_peer, device_id_type=MESH)
    for d in range(1, n_g):
        pl.semaphore_signal(barrier, inc=1, device_id=g_peer(d), device_id_type=MESH)
    pl.semaphore_wait(barrier, n_x - 1 + 1 + n_g - 1)

    def x_gather(buf, which, c, d):
        at = rows(share * block + c * half, half)
        return remote(buf.at[at], buf.at[at], gx_sems, (which, c, d - 1), x_peer(d))

    def core_gather(buf, which, c, d):
        at = rows(share_at(d, False) * block + c * half, half)
        return remote(buf.at[at], buf.at[at], gc_sems, (which, c, d), core_peer)

    gathered[rows(share * block, block), :] = embeds[...]
    for c in range(2):
        for d in range(1, n_x):
            x_gather(gathered, 0, c, d).start()
        core_gather(gathered, 0, c, 0).start()

    def id_copy(d):
        return remote(ids.at[me], ids.at[me], id_sems, (d - 1,), g_peer(d))

    ids[me] = ids_row[...]
    for d in range(1, n_g):
        id_copy(d).start()

    def product(j, c):
        at = rows(j * block + c * half, half)
        value = jnp.dot(gathered[at, :], w_first[...], preferred_element_type=jnp.float32)
        pre[at, :] = value
        value = gelu_fwd(value).astype(jnp.bfloat16)
        hidden[at, :] = value
        value = jnp.dot(value, w_second[...], preferred_element_type=jnp.float32)
        return value.astype(jnp.bfloat16)

    def core_sum(d, c):
        return remote(core_out.at[d, c], core_in.at[d, c], pc_sems, (d, c), core_peer)

    def x_sum(d, c):
        device = {"dp": share_at(d, False)}
        return remote(x_out.at[d - 1, c], x_in.at[d - 1, c], px_sems, (d - 1, c), device)

    for c in range(2):
        kept[rows(c * half, half), :] = product(share, c).astype(jnp.float32)
    for c in range(2):
        core_gather(gathered, 0, c, 0).wait_recv()
        core_out[0, c] = product(share_at(0, True), c)
        core_sum(0, c).start()
    for c in range(2):
        for d in range(1, n_x):
            x_gather(gathered, 0, c, d).wait_recv()
            core_gather(gathered, 0, c, d).start()
        for d in range(1, n_x):
            own = product(share_at(d, False), c).astype(jnp.float32)
            core_gather(gathered, 0, c, d).wait_recv()
            core_out[d, c] = product(share_at(d, True), c)
            core_sum(d, c).start()
            core_sum(d, c).wait_recv()
            own = own + core_in[d, c].astype(jnp.float32)
            x_out[d - 1, c] = own.astype(jnp.bfloat16)
            x_sum(d, c).start()

    def z_gather(p, d):
        at = rows(p * part, part)
        return remote(units.at[me, at], units.at[me, at], uz_sems, (p, d - 1), z_peer(d))

    def y_gather(p, dz, d):
        b, at = owner_at(dz, 0), rows(p * part, part)
        return remote(units.at[b, at], units.at[b, at], uy_sems, (p, dz, d - 1), y_peer(d))

    for c in range(2):
        at = rows(c * half, half)
        core_sum(0, c).wait_recv()
        proj = kept[at, :] + core_in[0, c].astype(jnp.float32)
        for d in range(1, n_x):
            x_sum(d, c).wait_recv()
            proj = proj + x_in[d - 1, c].astype(jnp.float32)
        inv = lax.rsqrt(jnp.mean(proj * proj, axis=-1, keepdims=True) + EPS)
        value = proj * inv
        inverse[at, :] = jnp.broadcast_to(inv, (half, LANES))
        unit[at, :] = value
        units[me, at, :] = value.astype(jnp.bfloat16)
        for p in range(c * UNIT_PARTS // 2, (c + 1) * UNIT_PARTS // 2):
            for d in range(1, n_z):
                z_gather(p, d).start()
            for d in range(1, n_y):
                y_gather(p, 0, d).start()

    for d in range(1, n_g):
        id_copy(d).wait_recv()
    grad_unit[...] = jnp.zeros(grad_unit.shape, jnp.float32)

    def add_block(b):
        logits = (
            TEMP
            / width_of(units)
            * lax.dot_general(
                units[me], units[b], (((1,), (1,)), ((), ())), preferred_element_type=jnp.float32
            )
            + SHIFT
        )
        sign = jnp.where(ids_col[...] == ids[b][0:1, :], 1.0, -1.0).astype(jnp.float32)
        weight = (-sign * jax.nn.sigmoid(-sign * logits) * (TEMP / width_of(units))).astype(
            jnp.bfloat16
        )
        weight = (weight.astype(jnp.float32) * times[b][0:1, 0:1]).astype(jnp.bfloat16)
        grad_unit[...] += jnp.dot(weight, units[b], preferred_element_type=jnp.float32)

    add_block(me)

    @pl.loop(0, n_x * 2)
    def _(j):
        at = rows(j * block, block)
        gathered_t[:, at] = gathered[at, :].T

    for p in range(UNIT_PARTS):
        for dz in range(1, n_z):
            z_gather(p, dz).wait_recv()
            for d in range(1, n_y):
                y_gather(p, dz, d).start()

    @pl.loop(1, n_z)
    def _(dz):
        add_block(owner_at(dz, 0))

    for dy in range(1, n_y):
        for p in range(UNIT_PARTS):
            y_gather(p, 0, dy).wait_recv()
        add_block(owner_at(0, dy))

        @pl.loop(1, n_z)
        def _(dz, dy=dy):
            for p in range(UNIT_PARTS):
                y_gather(p, dz, dy).wait_recv()
            add_block(owner_at(dz, dy))

    for c in range(2):
        at = rows(c * half, half)
        total, value = grad_unit[at, :], unit[at, :]
        slope = jnp.mean(value * total, axis=-1, keepdims=True)
        grad = inverse[at, 0:1] * (total - value * slope)
        grad_all[rows(share * block + c * half, half), :] = grad.astype(jnp.bfloat16)
        for d in range(1, n_x):
            x_gather(grad_all, 1, c, d).start()
        core_gather(grad_all, 1, c, 0).start()

    def hand_out(j):
        at = rows(j * block, block)
        value = grad_all[at, :]
        grads[at, :] = value
        grads_t[:, at] = value.T

    hand_out(share)
    for c in range(2):
        for d in range(1, n_x):
            x_gather(grad_all, 1, c, d).wait_recv()
            core_gather(grad_all, 1, c, d).start()
    for d in range(n_x):
        if d > 0:
            hand_out(share_at(d, False))
        for c in range(2):
            core_gather(grad_all, 1, c, d).wait_recv()
        hand_out(share_at(d, True))

    for d in range(1, n_g):
        id_copy(d).wait_send()
    for c in range(2):
        for which, buf in enumerate((gathered, grad_all)):
            for d in range(1, n_x):
                x_gather(buf, which, c, d).wait_send()
            for d in range(n_x):
                core_gather(buf, which, c, d).wait_send()
        for d in range(n_x):
            core_sum(d, c).wait_send()
        for d in range(1, n_x):
            x_sum(d, c).wait_send()

    for p in range(UNIT_PARTS):
        for d in range(1, n_z):
            z_gather(p, d).wait_send()
        for d in range(1, n_y):
            for dz in range(n_z):
                y_gather(p, dz, d).wait_send()


def width_of(units):
    return units.shape[-1]


def front(embeds, row_ids, times, w_first, w_second):
    owners, shares = lax.axis_size("group"), lax.axis_size("dp")
    n_y = split(owners, shares)
    n_z, n_x = owners // n_y, shares // 2
    block, wide = embeds.shape
    total, hid, width = shares * block, w_second.shape[0], w_second.shape[1]
    half = block // 2
    vmem = pl.BlockSpec(memory_space=pltpu.VMEM)
    dma = pltpu.SemaphoreType.DMA
    bf16, f32 = jnp.bfloat16, jnp.float32
    return pl.pallas_call(
        functools.partial(front_kernel, n_x, n_y, n_z),
        out_shape=[
            jax.ShapeDtypeStruct((wide, total), bf16),
            jax.ShapeDtypeStruct((total, hid), f32),
            jax.ShapeDtypeStruct((total, hid), bf16),
            jax.ShapeDtypeStruct((block, width), f32),
            jax.ShapeDtypeStruct((total, width), bf16),
            jax.ShapeDtypeStruct((width, total), bf16),
        ],
        in_specs=[vmem] * 6,
        out_specs=[vmem] * 6,
        scratch_shapes=[
            pltpu.VMEM((total, wide), bf16),
            pltpu.VMEM((owners, 8, block), jnp.int32),
            pltpu.VMEM((owners, block, width), bf16),
            pltpu.VMEM((block, width), f32),
            pltpu.VMEM((block, LANES), f32),
            pltpu.VMEM((total, width), bf16),
            pltpu.VMEM((n_x, 2, half, width), bf16),
            pltpu.VMEM((n_x, 2, half, width), bf16),
            pltpu.VMEM((n_x - 1, 2, half, width), bf16),
            pltpu.VMEM((n_x - 1, 2, half, width), bf16),
            pltpu.VMEM((block, width), f32),
            dma((2, owners - 1)),
            dma((2, 2, 2, n_x - 1)),
            dma((2, 2, 2, n_x)),
            dma((2, n_x, 2)),
            dma((2, n_x - 1, 2)),
            dma((2, UNIT_PARTS, n_z - 1)),
            dma((2, UNIT_PARTS, n_z, n_y - 1)),
        ],
        compiler_params=pltpu.CompilerParams(
            collective_id=1, has_side_effects=True, vmem_limit_bytes=VMEM_BYTES
        ),
    )(
        embeds,
        row_ids[:, None],
        jnp.broadcast_to(row_ids[None, :], (8, block)),
        jnp.broadcast_to(times[:, None, None], (owners, 8, LANES)),
        w_first,
        w_second,
    )


def per_device(embeds, row_ids, neighbors, w_first, w_second):
    owners = lax.axis_size("group")
    me = lax.axis_index("group")
    others = jnp.arange(owners, dtype=jnp.int32)
    mine = lax.dynamic_index_in_dim(neighbors, me, 0, keepdims=False)
    lists = jnp.sum((mine[None, :] == others[:, None]).astype(jnp.float32), axis=1)
    listed_by = jnp.sum((neighbors == me).astype(jnp.float32), axis=1)
    times = jnp.where(others == me, 2.0, lists + listed_by)
    gathered_t, pre, hidden, grad_unit, grads, grads_t = front(
        embeds, row_ids, times, w_first, w_second
    )
    sums = weight_sums(grads_t, gathered_t, hidden, pre, grads, w_second)
    return (sums[1], sums[0].T, grad_unit)


def solution(mesh):
    in_specs = (
        P(("dp", "group"), None),
        P(("dp", "group")),
        P("dp", None),
        P(None, "dp"),
        P("dp", None),
    )
    out_specs = (P("group", "dp"), P("dp", "group"), P(("dp", "group"), None))
    return jax.shard_map(
        per_device, mesh=mesh, in_specs=in_specs, out_specs=out_specs, check_vma=False
    )
```

profile of v0, /device:TPU:0, one launch (start us, length us, event | category | flops | bytes accessed | tf_op | source)
XLA Modules:
  0.0 180.1 jit_solution(11305845360005791414)
XLA Ops:
  0.6 0.9 dynamic-slice_reduce_fusion
  1.5 0.8 convert_reduce_fusion
  2.3 1.3 broadcast_in_dim.11.ids_row
  3.6 0.7 broadcast_in_dim.24.times
  4.2 1.5 copy.11.ids_col
  5.7 101.3 %shard_map.76 = (bf16[1024,1024]{1,0:T(8,128)(2,1)}, f32[1024,1024]{1,0:T(8,128)}, bf16[1024,1024]{1,0:T(8,128)(2,1)}, f32[256,1024]{1,0:T(8,128)}, bf16[1024,10...) custom-call(bf16[256,1024]{1,0:T(8,128)(2,1)} %embeds.1, s32[256,1]{1,0:T(8,128)} %copy.11.ids_col, ...), custom_call_target="tpu_custom_call" | custom-call | tf_op jit(solution)/shard_map/pallas_call | solution.py:513
  107.0 69.0 %shard_map.77 = f32[2,128,1024]{2,1,0:T(8,128)} custom-call(bf16[1024,1024]{1,0:T(8,128)(2,1)} %get-tuple-element.9.left0, bf16[1024,1024]{1,0:T(8,128)(2,1)} %get-tuple-element.10.left1, bf16[1024,1024]{1,0:T(8,128)(2,1)} %get-tuple-element.11.hidden, f32[1024,1024]{1,0:T(8,128)} %get-tuple-element.12.pre, bf16[1024,1024]{1,0:T(8,128)(2,1)} %get-tuple-element.13.grads, ...), custom_call_target="tpu_custom_call" | custom-call | tf_op jit(solution)/shard_map/pallas_call | solution.py:209
  176.0 0.0 copy-start
  176.0 2.2 %slice_bitcast_fusion = (f32[1024,128]{0,1:T(8,128)S(1)}, f32[128,1024]{1,0:T(8,128)}) fusion(f32[2,128,1024]{2,1,0:T(8,128)} %shard_map.77), kind=kLoop, calls=%fused_computation | loop fusion | bytes 2097152 | tf_op jit(solution)/shard_map/transpose | solution.py:570
  178.1 1.0 copy.12
  179.1 0.0 copy-done
  179.1 1.0 copy.14
  (1 shorter events, 0.0 us)
Async XLA Ops:
  176.0 3.2 %copy-start = (f32[256,1024]{1,0:T(8,128)S(1)}, f32[256,1024]{1,0:T(8,128)}, u32[]{:S(2)}) copy-start(f32[256,1024]{1,0:T(8,128)} %get-tuple-element.33) | copy-start | bytes 3145732
where the time goes:
time: 180 us
  Pallas kernels  170 us (94%)
  local copies, waits for them, and re-layouts  8.45 us (5%)
    pallas_call x1, Pallas kernels, front(): pl.pallas_call(functools.partial(front_kernel, n_x, n_y, n_z), out_shape=...  101 us
    pallas_call x1, Pallas kernels, weight_sums(): pl.pallas_call(functools.partial(weight_kernel, n_y, n_z), out_shape=jax....  69 us

commit v1 on v0

--- a/solution.py
+++ b/solution.py
@@ -14,7 +14,7 @@
 LANES = 128
 CHUNK = 256
 UNIT_PARTS = 4
-VMEM_BYTES = 60 * 1024 * 1024
+VMEM_BYTES = 63 * 1024 * 1024
 MESH = pl.DeviceIdType.MESH
 
 
@@ -44,7 +44,7 @@
     return code.astype(jnp.int32).astype(jnp.float32) * wide
 
 
-def weight_kernel(
+def weight_part(
     n_y,
     n_z,
     left0,
@@ -53,7 +53,8 @@
     pre,
     grads,
     w_second,
-    out,
+    first,
+    second,
     grad_pre,
     own,
     mine,
@@ -70,8 +71,8 @@
 ):
     me = lax.axis_index("group")
     z, y = me // n_y, me % n_y
-    tall = out.shape[1]
-    chunks = out.shape[2] // CHUNK
+    tall = first.shape[0]
+    chunks = first.shape[1] // CHUNK
 
     def y_peer(d):
         return z * n_y + lax.rem(y + d, n_y)
@@ -104,13 +105,6 @@
             )
             for which, (a, b) in enumerate(((z_out, z_in), (z_scale_out, z_scale_in)))
         ]
-
-    barrier = pltpu.get_barrier_semaphore()
-    for d in range(1, n_y):
-        pl.semaphore_signal(barrier, inc=1, device_id={"group": y_peer(d)}, device_id_type=MESH)
-    for d in range(1, n_z):
-        pl.semaphore_signal(barrier, inc=1, device_id={"group": z_peer(d)}, device_id_type=MESH)
-    pl.semaphore_wait(barrier, n_y + n_z - 2)
 
     def send_partials(i, left, rhs):
         def partial(owner_y, row):
@@ -182,7 +176,11 @@
                     copy.wait_recv()
             for d in range(1, n_z):
                 block = block + decode(z_in[i, d - 1], z_scale_in[i, d - 1])
-            out[m, :, pl.ds(pl.multiple_of(k * CHUNK, CHUNK), CHUNK)] = block
+            at = pl.ds(pl.multiple_of(k * CHUNK, CHUNK), CHUNK)
+            if m == 0:
+                second[at, :] = block.T
+            else:
+                first[:, at] = block
 
     @pl.loop(0, 2 * chunks)
     def _(i):
@@ -198,56 +196,23 @@
     return shares // 2 if owners % (shares // 2) == 0 else 1
 
 
-def weight_sums(left0, left1, hidden, pre, grads, w_second):
-    owners, shares = lax.axis_size("group"), lax.axis_size("dp")
-    n_y = split(owners, shares)
-    n_z = owners // n_y
-    tall = left0.shape[0] // owners
-    wide = hidden.shape[1]
-    items = 2 * (wide // CHUNK)
-    vmem = pl.BlockSpec(memory_space=pltpu.VMEM)
-    return pl.pallas_call(
-        functools.partial(weight_kernel, n_y, n_z),
-        out_shape=jax.ShapeDtypeStruct((2, tall, wide), jnp.float32),
-        in_specs=[vmem] * 6,
-        out_specs=vmem,
-        scratch_shapes=[
-            pltpu.VMEM((hidden.shape[0], CHUNK), jnp.bfloat16),
-            pltpu.VMEM((items, n_z, tall, CHUNK), jnp.float32),
-            pltpu.VMEM((items, tall, CHUNK), jnp.float32),
-            pltpu.VMEM((items, n_y - 1, n_z, tall, CHUNK), jnp.int16),
-            pltpu.VMEM((items, n_y - 1, n_z, tall, CHUNK), jnp.int16),
-            pltpu.VMEM((items, n_y - 1, 8, LANES), jnp.float32),
-            pltpu.VMEM((items, n_y - 1, 8, LANES), jnp.float32),
-            pltpu.VMEM((items, n_z - 1, tall, CHUNK), jnp.int16),
-            pltpu.VMEM((items, n_z - 1, tall, CHUNK), jnp.int16),
-            pltpu.VMEM((items, n_z - 1, 8, LANES), jnp.float32),
-            pltpu.VMEM((items, n_z - 1, 8, LANES), jnp.float32),
-            pltpu.SemaphoreType.DMA((2, 2, items, n_y - 1)),
-            pltpu.SemaphoreType.DMA((2, 2, items, n_z - 1)),
-        ],
-        compiler_params=pltpu.CompilerParams(
-            collective_id=0, has_side_effects=True, vmem_limit_bytes=VMEM_BYTES
-        ),
-    )(left0, left1, hidden, pre, grads, w_second)
-
-
-def front_kernel(
+def step_kernel(
     n_x,
     n_y,
     n_z,
     embeds,
-    ids_col,
-    ids_row,
-    times,
+    own_ids,
+    neighbors,
     w_first,
     w_second,
+    first,
+    second,
+    grad_unit,
     gathered_t,
     pre,
     hidden,
-    grad_unit,
-    grads,
     grads_t,
+    ids_col,
     gathered,
     ids,
     units,
@@ -258,7 +223,6 @@
     core_in,
     x_out,
     x_in,
-    kept,
     id_sems,
     gx_sems,
     gc_sems,
@@ -266,6 +230,7 @@
     px_sems,
     uz_sems,
     uy_sems,
+    *weight_scratch,
 ):
     share, me = lax.axis_index("dp"), lax.axis_index("group")
     x, core = share // 2, share % 2
@@ -333,12 +298,12 @@
     def id_copy(d):
         return remote(ids.at[me], ids.at[me], id_sems, (d - 1,), g_peer(d))
 
-    ids[me] = ids_row[...]
+    ids[me] = jnp.broadcast_to(own_ids[...], ids.shape[1:])
     for d in range(1, n_g):
         id_copy(d).start()
 
-    def product(j, c):
-        at = rows(j * block + c * half, half)
+    def product(j, c, count):
+        at = rows(j * block + c * half, count)
         value = jnp.dot(gathered[at, :], w_first[...], preferred_element_type=jnp.float32)
         pre[at, :] = value
         value = gelu_fwd(value).astype(jnp.bfloat16)
@@ -353,20 +318,20 @@
         device = {"dp": share_at(d, False)}
         return remote(x_out.at[d - 1, c], x_in.at[d - 1, c], px_sems, (d - 1, c), device)
 
-    for c in range(2):
-        kept[rows(c * half, half), :] = product(share, c).astype(jnp.float32)
+    unit[...] = product(share, 0, block).astype(jnp.float32)
     for c in range(2):
         core_gather(gathered, 0, c, 0).wait_recv()
-        core_out[0, c] = product(share_at(0, True), c)
+    core_out[0] = product(share_at(0, True), 0, block).reshape(core_out.shape[1:])
+    for c in range(2):
         core_sum(0, c).start()
     for c in range(2):
         for d in range(1, n_x):
             x_gather(gathered, 0, c, d).wait_recv()
             core_gather(gathered, 0, c, d).start()
         for d in range(1, n_x):
-            own = product(share_at(d, False), c).astype(jnp.float32)
+            own = product(share_at(d, False), c, half).astype(jnp.float32)
             core_gather(gathered, 0, c, d).wait_recv()
-            core_out[d, c] = product(share_at(d, True), c)
+            core_out[d, c] = product(share_at(d, True), c, half)
             core_sum(d, c).start()
             core_sum(d, c).wait_recv()
             own = own + core_in[d, c].astype(jnp.float32)
@@ -384,7 +349,7 @@
     for c in range(2):
         at = rows(c * half, half)
         core_sum(0, c).wait_recv()
-        proj = kept[at, :] + core_in[0, c].astype(jnp.float32)
+        proj = unit[at, :] + core_in[0, c].astype(jnp.float32)
         for d in range(1, n_x):
             x_sum(d, c).wait_recv()
             proj = proj + x_in[d - 1, c].astype(jnp.float32)
@@ -402,6 +367,7 @@
     for d in range(1, n_g):
         id_copy(d).wait_recv()
     grad_unit[...] = jnp.zeros(grad_unit.shape, jnp.float32)
+    ids_col[...] = ids[me].T
 
     def add_block(b):
         logits = (
@@ -412,11 +378,15 @@
             )
             + SHIFT
         )
-        sign = jnp.where(ids_col[...] == ids[b][0:1, :], 1.0, -1.0).astype(jnp.float32)
+        sign = jnp.where(ids_col[:, 0:1] == ids[b][0:1, :], 1.0, -1.0).astype(jnp.float32)
         weight = (-sign * jax.nn.sigmoid(-sign * logits) * (TEMP / width_of(units))).astype(
             jnp.bfloat16
         )
-        weight = (weight.astype(jnp.float32) * times[b][0:1, 0:1]).astype(jnp.bfloat16)
+        lists = (neighbors[pl.ds(me, 1), :] == b).astype(jnp.float32)
+        listed_by = (neighbors[pl.ds(b, 1), :] == me).astype(jnp.float32)
+        times = jnp.sum(lists + listed_by, axis=1, keepdims=True)
+        times = jnp.where(b == me, 2.0, times)
+        weight = (weight.astype(jnp.float32) * times).astype(jnp.bfloat16)
         grad_unit[...] += jnp.dot(weight, units[b], preferred_element_type=jnp.float32)
 
     add_block(me)
@@ -459,9 +429,7 @@
 
     def hand_out(j):
         at = rows(j * block, block)
-        value = grad_all[at, :]
-        grads[at, :] = value
-        grads_t[:, at] = value.T
+        grads_t[:, at] = grad_all[at, :].T
 
     hand_out(share)
     for c in range(2):
@@ -475,6 +443,20 @@
             core_gather(grad_all, 1, c, d).wait_recv()
         hand_out(share_at(d, True))
 
+    weight_part(
+        n_y,
+        n_z,
+        grads_t,
+        gathered_t,
+        hidden,
+        pre,
+        grad_all,
+        w_second,
+        first,
+        second,
+        *weight_scratch,
+    )
+
     for d in range(1, n_g):
         id_copy(d).wait_send()
     for c in range(2):
@@ -500,29 +482,32 @@
     return units.shape[-1]
 
 
-def front(embeds, row_ids, times, w_first, w_second):
+def step(embeds, row_ids, neighbors, w_first, w_second):
     owners, shares = lax.axis_size("group"), lax.axis_size("dp")
     n_y = split(owners, shares)
     n_z, n_x = owners // n_y, shares // 2
     block, wide = embeds.shape
     total, hid, width = shares * block, w_second.shape[0], w_second.shape[1]
-    half = block // 2
+    half, tall = block // 2, wide // owners
+    items = 2 * (hid // CHUNK)
     vmem = pl.BlockSpec(memory_space=pltpu.VMEM)
     dma = pltpu.SemaphoreType.DMA
-    bf16, f32 = jnp.bfloat16, jnp.float32
+    bf16, f32, i16 = jnp.bfloat16, jnp.float32, jnp.int16
     return pl.pallas_call(
-        functools.partial(front_kernel, n_x, n_y, n_z),
+        functools.partial(step_kernel, n_x, n_y, n_z),
         out_shape=[
-            jax.ShapeDtypeStruct((wide, total), bf16),
-            jax.ShapeDtypeStruct((total, hid), f32),
-            jax.ShapeDtypeStruct((total, hid), bf16),
+            jax.ShapeDtypeStruct((tall, hid), f32),
+            jax.ShapeDtypeStruct((hid, tall), f32),
             jax.ShapeDtypeStruct((block, width), f32),
-            jax.ShapeDtypeStruct((total, width), bf16),
-            jax.ShapeDtypeStruct((width, total), bf16),
         ],
-        in_specs=[vmem] * 6,
-        out_specs=[vmem] * 6,
+        in_specs=[vmem] * 5,
+        out_specs=[vmem] * 3,
         scratch_shapes=[
+            pltpu.VMEM((wide, total), bf16),
+            pltpu.VMEM((total, hid), f32),
+            pltpu.VMEM((total, hid), bf16),
+            pltpu.VMEM((width, total), bf16),
+            pltpu.VMEM((block, 8), jnp.int32),
             pltpu.VMEM((total, wide), bf16),
             pltpu.VMEM((owners, 8, block), jnp.int32),
             pltpu.VMEM((owners, block, width), bf16),
@@ -533,7 +518,6 @@
             pltpu.VMEM((n_x, 2, half, width), bf16),
             pltpu.VMEM((n_x - 1, 2, half, width), bf16),
             pltpu.VMEM((n_x - 1, 2, half, width), bf16),
-            pltpu.VMEM((block, width), f32),
             dma((2, owners - 1)),
             dma((2, 2, 2, n_x - 1)),
             dma((2, 2, 2, n_x)),
@@ -541,33 +525,28 @@
             dma((2, n_x - 1, 2)),
             dma((2, UNIT_PARTS, n_z - 1)),
             dma((2, UNIT_PARTS, n_z, n_y - 1)),
+            pltpu.VMEM((total, CHUNK), bf16),
+            pltpu.VMEM((items, n_z, tall, CHUNK), f32),
+            pltpu.VMEM((items, tall, CHUNK), f32),
+            pltpu.VMEM((items, n_y - 1, n_z, tall, CHUNK), i16),
+            pltpu.VMEM((items, n_y - 1, n_z, tall, CHUNK), i16),
+            pltpu.VMEM((items, n_y - 1, 8, LANES), f32),
+            pltpu.VMEM((items, n_y - 1, 8, LANES), f32),
+            pltpu.VMEM((items, n_z - 1, tall, CHUNK), i16),
+            pltpu.VMEM((items, n_z - 1, tall, CHUNK), i16),
+            pltpu.VMEM((items, n_z - 1, 8, LANES), f32),
+            pltpu.VMEM((items, n_z - 1, 8, LANES), f32),
+            dma((2, 2, items, n_y - 1)),
+            dma((2, 2, items, n_z - 1)),
         ],
         compiler_params=pltpu.CompilerParams(
-            collective_id=1, has_side_effects=True, vmem_limit_bytes=VMEM_BYTES
+            collective_id=0, has_side_effects=True, vmem_limit_bytes=VMEM_BYTES
         ),
-    )(
-        embeds,
-        row_ids[:, None],
-        jnp.broadcast_to(row_ids[None, :], (8, block)),
-        jnp.broadcast_to(times[:, None, None], (owners, 8, LANES)),
-        w_first,
-        w_second,
-    )
+    )(embeds, row_ids[None, :], neighbors, w_first, w_second)
 
 
 def per_device(embeds, row_ids, neighbors, w_first, w_second):
-    owners = lax.axis_size("group")
-    me = lax.axis_index("group")
-    others = jnp.arange(owners, dtype=jnp.int32)
-    mine = lax.dynamic_index_in_dim(neighbors, me, 0, keepdims=False)
-    lists = jnp.sum((mine[None, :] == others[:, None]).astype(jnp.float32), axis=1)
-    listed_by = jnp.sum((neighbors == me).astype(jnp.float32), axis=1)
-    times = jnp.where(others == me, 2.0, lists + listed_by)
-    gathered_t, pre, hidden, grad_unit, grads, grads_t = front(
-        embeds, row_ids, times, w_first, w_second
-    )
-    sums = weight_sums(grads_t, gathered_t, hidden, pre, grads, w_second)
-    return (sums[1], sums[0].T, grad_unit)
+    return tuple(step(embeds, row_ids, neighbors, w_first, w_second))
 
 
 def solution(mesh):

time: 180 us -> 164 us (0.911)
  Pallas kernels: 170 us -> 156 us
  local copies, waits for them, and re-layouts: 8.45 us -> 6.16 us
    pallas_call x2 -> x1, Pallas kernels: 170 us -> 156 us  [step(): pl.pallas_call(functools.partial(step_kernel, n_x, n_y, n_z), out_shape=[...]
    unnamed x4 -> x6, local copies, waits for them, and re-layouts: 1.97 us -> 6.16 us
    broadcast_in_dim x3 -> x0, local copies, waits for them, and re-layouts: 3.44 us -> none  [the longest x1 1.47 us: front(): row_ids[:, None]]
    transpose x1 -> x0, local copies, waits for them, and re-layouts: 2.17 us -> none  [per_device(): return (sums[1], sums[0].T, grad_unit)]
where the time goes in v1:
time: 164 us; the launch traced here: 162 us
  Pallas kernels  156 us (95%)
  local copies, waits for them, and re-layouts  6.16 us (4%)
    pallas_call x1, Pallas kernels, step(): pl.pallas_call(functools.partial(step_kernel, n_x, n_y, n_z), out_shape=[...  156 us
    unnamed x6, local copies, waits for them, and re-layouts  6.16 us

profile of v1, /device:TPU:0, one launch (start us, length us, event | category | flops | bytes accessed | tf_op | source)
XLA Modules:
  0.0 162.4 jit_solution(9416518237510378590)
XLA Ops:
  0.6 1.3 copy.8.neighbors
  2.0 155.6 %shard_map.76 = (f32[128,1024]{1,0:T(8,128)}, f32[1024,128]{1,0:T(8,128)}, f32[256,1024]{1,0:T(8,128)}) custom-call(bf16[256,1024]{1,0:T(8,128)(2,1)} %embeds.1, s32[1,256]{1,0:T(1,128)} %bitcast.1, s32[8,3]{1,0:T(8,128)} %copy.8.neighbors, bf16[1024,1024]{1,0:T(8,128)(2,1)} %w_first.1, bf16[1024,1024]{1,0:T(8,128)(2,1)} %w_second.1), custom_call_target="tpu_custom_call" | custom-call | tf_op jit(solution)/shard_map/pallas_call | solution.py:496
  157.5 0.0 copy-start
  157.6 2.0 %copy.12 = f32[128,1024]{1,0:T(8,128)} copy(f32[128,1024]{1,0:T(8,128)} %get-tuple-element.6) | data formatting | bytes 1048576
  159.5 1.9 %copy.13 = f32[1024,128]{1,0:T(8,128)} copy(f32[1024,128]{1,0:T(8,128)} %get-tuple-element.7) | data formatting | bytes 1048576
  161.4 0.0 copy-done
  161.4 1.0 copy.14
Async XLA Ops:
  157.5 3.9 %copy-start = (f32[256,1024]{1,0:T(8,128)S(1)}, f32[256,1024]{1,0:T(8,128)}, u32[]{:S(2)}) copy-start(f32[256,1024]{1,0:T(8,128)} %get-tuple-element.8) | copy-start | bytes 3145732

commit v2 on v1

--- a/solution.py
+++ b/solution.py
@@ -13,7 +13,7 @@
 LEVELS = 32000.0
 LANES = 128
 CHUNK = 256
-UNIT_PARTS = 4
+PARTS = 4
 VMEM_BYTES = 63 * 1024 * 1024
 MESH = pl.DeviceIdType.MESH
 
@@ -236,8 +236,7 @@
     x, core = share // 2, share % 2
     z, y = me // n_y, me % n_y
     block, width = embeds.shape
-    half = block // 2
-    part = block // UNIT_PARTS
+    part = block // PARTS
     n_g = n_y * n_z
 
     def remote(src, dst, sems, at, device):
@@ -282,15 +281,15 @@
     pl.semaphore_wait(barrier, n_x - 1 + 1 + n_g - 1)
 
     def x_gather(buf, which, c, d):
-        at = rows(share * block + c * half, half)
+        at = rows(share * block + c * part, part)
         return remote(buf.at[at], buf.at[at], gx_sems, (which, c, d - 1), x_peer(d))
 
     def core_gather(buf, which, c, d):
-        at = rows(share_at(d, False) * block + c * half, half)
+        at = rows(share_at(d, False) * block + c * part, part)
         return remote(buf.at[at], buf.at[at], gc_sems, (which, c, d), core_peer)
 
     gathered[rows(share * block, block), :] = embeds[...]
-    for c in range(2):
+    for c in range(PARTS):
         for d in range(1, n_x):
             x_gather(gathered, 0, c, d).start()
         core_gather(gathered, 0, c, 0).start()
@@ -302,13 +301,15 @@
     for d in range(1, n_g):
         id_copy(d).start()
 
-    def product(j, c, count):
-        at = rows(j * block + c * half, count)
-        value = jnp.dot(gathered[at, :], w_first[...], preferred_element_type=jnp.float32)
-        pre[at, :] = value
-        value = gelu_fwd(value).astype(jnp.bfloat16)
-        hidden[at, :] = value
-        value = jnp.dot(value, w_second[...], preferred_element_type=jnp.float32)
+    def product(*places):
+        value = jnp.concatenate([gathered[at, :] for at in places], 0)
+        value = jnp.dot(value, w_first[...], preferred_element_type=jnp.float32)
+        active = gelu_fwd(value).astype(jnp.bfloat16)
+        count = value.shape[0] // len(places)
+        for k, at in enumerate(places):
+            pre[at, :] = value[k * count : (k + 1) * count]
+            hidden[at, :] = active[k * count : (k + 1) * count]
+        value = jnp.dot(active, w_second[...], preferred_element_type=jnp.float32)
         return value.astype(jnp.bfloat16)
 
     def core_sum(d, c):
@@ -318,26 +319,6 @@
         device = {"dp": share_at(d, False)}
         return remote(x_out.at[d - 1, c], x_in.at[d - 1, c], px_sems, (d - 1, c), device)
 
-    unit[...] = product(share, 0, block).astype(jnp.float32)
-    for c in range(2):
-        core_gather(gathered, 0, c, 0).wait_recv()
-    core_out[0] = product(share_at(0, True), 0, block).reshape(core_out.shape[1:])
-    for c in range(2):
-        core_sum(0, c).start()
-    for c in range(2):
-        for d in range(1, n_x):
-            x_gather(gathered, 0, c, d).wait_recv()
-            core_gather(gathered, 0, c, d).start()
-        for d in range(1, n_x):
-            own = product(share_at(d, False), c, half).astype(jnp.float32)
-            core_gather(gathered, 0, c, d).wait_recv()
-            core_out[d, c] = product(share_at(d, True), c, half)
-            core_sum(d, c).start()
-            core_sum(d, c).wait_recv()
-            own = own + core_in[d, c].astype(jnp.float32)
-            x_out[d - 1, c] = own.astype(jnp.bfloat16)
-            x_sum(d, c).start()
-
     def z_gather(p, d):
         at = rows(p * part, part)
         return remote(units.at[me, at], units.at[me, at], uz_sems, (p, d - 1), z_peer(d))
@@ -346,8 +327,8 @@
         b, at = owner_at(dz, 0), rows(p * part, part)
         return remote(units.at[b, at], units.at[b, at], uy_sems, (p, dz, d - 1), y_peer(d))
 
-    for c in range(2):
-        at = rows(c * half, half)
+    def normalise(c):
+        at = rows(c * part, part)
         core_sum(0, c).wait_recv()
         proj = unit[at, :] + core_in[0, c].astype(jnp.float32)
         for d in range(1, n_x):
@@ -355,14 +336,48 @@
             proj = proj + x_in[d - 1, c].astype(jnp.float32)
         inv = lax.rsqrt(jnp.mean(proj * proj, axis=-1, keepdims=True) + EPS)
         value = proj * inv
-        inverse[at, :] = jnp.broadcast_to(inv, (half, LANES))
+        inverse[at, :] = jnp.broadcast_to(inv, (part, LANES))
         unit[at, :] = value
         units[me, at, :] = value.astype(jnp.bfloat16)
-        for p in range(c * UNIT_PARTS // 2, (c + 1) * UNIT_PARTS // 2):
-            for d in range(1, n_z):
-                z_gather(p, d).start()
-            for d in range(1, n_y):
-                y_gather(p, 0, d).start()
+        for d in range(1, n_z):
+            z_gather(c, d).start()
+        for d in range(1, n_y):
+            y_gather(c, 0, d).start()
+
+    def forward_embeds(c):
+        for d in range(1, n_x):
+            x_gather(gathered, 0, c, d).wait_recv()
+            core_gather(gathered, 0, c, d).start()
+
+    unit[...] = product(rows(share * block, block)).astype(jnp.float32)
+    forward_embeds(0)
+    for c in range(PARTS):
+        core_gather(gathered, 0, c, 0).wait_recv()
+    both = product(rows(share_at(0, True) * block, block))
+    core_out[0] = both.reshape(core_out.shape[1:])
+    for c in range(PARTS):
+        core_sum(0, c).start()
+    for c in range(PARTS):
+        kept = []
+        for d in range(1, n_x):
+            core_gather(gathered, 0, c, d).wait_recv()
+            both = product(
+                rows(share_at(d, True) * block + c * part, part),
+                rows(share_at(d, False) * block + c * part, part),
+            )
+            core_out[d, c] = both[:part]
+            core_sum(d, c).start()
+            kept.append(both[part:])
+        if c + 1 < PARTS:
+            forward_embeds(c + 1)
+        for d in range(1, n_x):
+            core_sum(d, c).wait_recv()
+            own = kept[d - 1].astype(jnp.float32) + core_in[d, c].astype(jnp.float32)
+            x_out[d - 1, c] = own.astype(jnp.bfloat16)
+            x_sum(d, c).start()
+        if c > 0:
+            normalise(c - 1)
+    normalise(PARTS - 1)
 
     for d in range(1, n_g):
         id_copy(d).wait_recv()
@@ -396,7 +411,7 @@
         at = rows(j * block, block)
         gathered_t[:, at] = gathered[at, :].T
 
-    for p in range(UNIT_PARTS):
+    for p in range(PARTS):
         for dz in range(1, n_z):
             z_gather(p, dz).wait_recv()
             for d in range(1, n_y):
@@ -407,22 +422,22 @@
         add_block(owner_at(dz, 0))
 
     for dy in range(1, n_y):
-        for p in range(UNIT_PARTS):
+        for p in range(PARTS):
             y_gather(p, 0, dy).wait_recv()
         add_block(owner_at(0, dy))
 
         @pl.loop(1, n_z)
         def _(dz, dy=dy):
-            for p in range(UNIT_PARTS):
+            for p in range(PARTS):
                 y_gather(p, dz, dy).wait_recv()
             add_block(owner_at(dz, dy))
 
-    for c in range(2):
-        at = rows(c * half, half)
+    for c in range(PARTS):
+        at = rows(c * part, part)
         total, value = grad_unit[at, :], unit[at, :]
         slope = jnp.mean(value * total, axis=-1, keepdims=True)
         grad = inverse[at, 0:1] * (total - value * slope)
-        grad_all[rows(share * block + c * half, half), :] = grad.astype(jnp.bfloat16)
+        grad_all[rows(share * block + c * part, part), :] = grad.astype(jnp.bfloat16)
         for d in range(1, n_x):
             x_gather(grad_all, 1, c, d).start()
         core_gather(grad_all, 1, c, 0).start()
@@ -432,14 +447,14 @@
         grads_t[:, at] = grad_all[at, :].T
 
     hand_out(share)
-    for c in range(2):
+    for c in range(PARTS):
         for d in range(1, n_x):
             x_gather(grad_all, 1, c, d).wait_recv()
             core_gather(grad_all, 1, c, d).start()
     for d in range(n_x):
         if d > 0:
             hand_out(share_at(d, False))
-        for c in range(2):
+        for c in range(PARTS):
             core_gather(grad_all, 1, c, d).wait_recv()
         hand_out(share_at(d, True))
 
@@ -459,7 +474,7 @@
 
     for d in range(1, n_g):
         id_copy(d).wait_send()
-    for c in range(2):
+    for c in range(PARTS):
         for which, buf in enumerate((gathered, grad_all)):
             for d in range(1, n_x):
                 x_gather(buf, which, c, d).wait_send()
@@ -470,7 +485,7 @@
         for d in range(1, n_x):
             x_sum(d, c).wait_send()
 
-    for p in range(UNIT_PARTS):
+    for p in range(PARTS):
         for d in range(1, n_z):
             z_gather(p, d).wait_send()
         for d in range(1, n_y):
@@ -488,7 +503,7 @@
     n_z, n_x = owners // n_y, shares // 2
     block, wide = embeds.shape
     total, hid, width = shares * block, w_second.shape[0], w_second.shape[1]
-    half, tall = block // 2, wide // owners
+    part, tall = block // PARTS, wide // owners
     items = 2 * (hid // CHUNK)
     vmem = pl.BlockSpec(memory_space=pltpu.VMEM)
     dma = pltpu.SemaphoreType.DMA
@@ -514,17 +529,17 @@
             pltpu.VMEM((block, width), f32),
             pltpu.VMEM((block, LANES), f32),
             pltpu.VMEM((total, width), bf16),
-            pltpu.VMEM((n_x, 2, half, width), bf16),
-            pltpu.VMEM((n_x, 2, half, width), bf16),
-            pltpu.VMEM((n_x - 1, 2, half, width), bf16),
-            pltpu.VMEM((n_x - 1, 2, half, width), bf16),
+            pltpu.VMEM((n_x, PARTS, part, width), bf16),
+            pltpu.VMEM((n_x, PARTS, part, width), bf16),
+            pltpu.VMEM((n_x - 1, PARTS, part, width), bf16),
+            pltpu.VMEM((n_x - 1, PARTS, part, width), bf16),
             dma((2, owners - 1)),
-            dma((2, 2, 2, n_x - 1)),
-            dma((2, 2, 2, n_x)),
-            dma((2, n_x, 2)),
-            dma((2, n_x - 1, 2)),
-            dma((2, UNIT_PARTS, n_z - 1)),
-            dma((2, UNIT_PARTS, n_z, n_y - 1)),
+            dma((2, 2, PARTS, n_x - 1)),
+            dma((2, 2, PARTS, n_x)),
+            dma((2, n_x, PARTS)),
+            dma((2, n_x - 1, PARTS)),
+            dma((2, PARTS, n_z - 1)),
+            dma((2, PARTS, n_z, n_y - 1)),
             pltpu.VMEM((total, CHUNK), bf16),
             pltpu.VMEM((items, n_z, tall, CHUNK), f32),
             pltpu.VMEM((items, tall, CHUNK), f32),

time: 164 us -> 161 us (0.982)
  Pallas kernels: 156 us -> 151 us
    pallas_call x1, Pallas kernels: 156 us -> 151 us  [step(): pl.pallas_call(functools.partial(step_kernel, n_x, n_y, n_z), out_shape=[...]
where the time goes in v2:
time: 161 us; the launch traced here: 158 us
  Pallas kernels  151 us (94%)
  local copies, waits for them, and re-layouts  6.16 us (4%)
    pallas_call x1, Pallas kernels, step(): pl.pallas_call(functools.partial(step_kernel, n_x, n_y, n_z), out_shape=[...  151 us
    unnamed x6, local copies, waits for them, and re-layouts  6.16 us

profile of v2, /device:TPU:0, one launch (start us, length us, event | category | flops | bytes accessed | tf_op | source)
XLA Modules:
  0.0 158.1 jit_solution(8398128757267926815)
XLA Ops:
  0.6 1.3 copy.8.neighbors
  2.0 151.3 %shard_map.76 = (f32[128,1024]{1,0:T(8,128)}, f32[1024,128]{1,0:T(8,128)}, f32[256,1024]{1,0:T(8,128)}) custom-call(bf16[256,1024]{1,0:T(8,128)(2,1)} %embeds.1, s32[1,256]{1,0:T(1,128)} %bitcast.1, s32[8,3]{1,0:T(8,128)} %copy.8.neighbors, bf16[1024,1024]{1,0:T(8,128)(2,1)} %w_first.1, bf16[1024,1024]{1,0:T(8,128)(2,1)} %w_second.1), custom_call_target="tpu_custom_call" | custom-call | tf_op jit(solution)/shard_map/pallas_call | solution.py:511
  153.3 0.0 copy-start
  153.3 2.0 %copy.12 = f32[128,1024]{1,0:T(8,128)} copy(f32[128,1024]{1,0:T(8,128)} %get-tuple-element.6) | data formatting | bytes 1048576
  155.2 1.9 %copy.13 = f32[1024,128]{1,0:T(8,128)} copy(f32[1024,128]{1,0:T(8,128)} %get-tuple-element.7) | data formatting | bytes 1048576
  157.1 0.0 copy-done
  157.1 1.0 copy.14
Async XLA Ops:
  153.3 3.9 %copy-start = (f32[256,1024]{1,0:T(8,128)S(1)}, f32[256,1024]{1,0:T(8,128)}, u32[]{:S(2)}) copy-start(f32[256,1024]{1,0:T(8,128)} %get-tuple-element.8) | copy-start | bytes 3145732

commit v3 on v2

--- a/solution.py
+++ b/solution.py
@@ -319,9 +319,36 @@
         device = {"dp": share_at(d, False)}
         return remote(x_out.at[d - 1, c], x_in.at[d - 1, c], px_sems, (d - 1, c), device)
 
-    def z_gather(p, d):
-        at = rows(p * part, part)
-        return remote(units.at[me, at], units.at[me, at], uz_sems, (p, d - 1), z_peer(d))
+    def line_copy(p, way, d):
+        source = z - (d - 1) if way == 0 else z + (d - 1)
+        to = lax.rem(z + (1 if way == 0 else n_z - 1), n_z)
+        b, at = source * n_y + y, rows(p * part, part)
+        device = {"group": to * n_y + y}
+        return remote(units.at[b, at], units.at[b, at], uz_sems, (way, p, d - 1), device)
+
+    def arrives(way, d):
+        return z >= d if way == 0 else z + d < n_z
+
+    def leaves(way, d):
+        if way == 0:
+            return jnp.logical_and(z >= d - 1, z + 1 < n_z)
+        return jnp.logical_and(z + d - 1 < n_z, z >= 1)
+
+    def relay(p):
+        for d in range(1, n_z):
+            for way in range(2):
+
+                @pl.when(arrives(way, d))
+                def _(d=d, way=way):
+                    line_copy(p, way, d).wait_recv()
+                    for e in range(1, n_y):
+                        y_gather(p, d if way == 0 else n_z - d, e).start()
+
+                if d + 1 < n_z:
+
+                    @pl.when(jnp.logical_and(arrives(way, d), leaves(way, d + 1)))
+                    def _(d=d, way=way):
+                        line_copy(p, way, d + 1).start()
 
     def y_gather(p, dz, d):
         b, at = owner_at(dz, 0), rows(p * part, part)
@@ -339,8 +366,12 @@
         inverse[at, :] = jnp.broadcast_to(inv, (part, LANES))
         unit[at, :] = value
         units[me, at, :] = value.astype(jnp.bfloat16)
-        for d in range(1, n_z):
-            z_gather(c, d).start()
+        for way in range(2):
+
+            @pl.when(leaves(way, 1))
+            def _(way=way):
+                line_copy(c, way, 1).start()
+
         for d in range(1, n_y):
             y_gather(c, 0, d).start()
 
@@ -404,18 +435,16 @@
         weight = (weight.astype(jnp.float32) * times).astype(jnp.bfloat16)
         grad_unit[...] += jnp.dot(weight, units[b], preferred_element_type=jnp.float32)
 
+    turns = -(-2 * n_x // PARTS)
+    for p in range(PARTS):
+        relay(p)
+
+        @pl.loop(p * turns, min((p + 1) * turns, 2 * n_x))
+        def _(j):
+            at = rows(j * block, block)
+            gathered_t[:, at] = gathered[at, :].T
+
     add_block(me)
-
-    @pl.loop(0, n_x * 2)
-    def _(j):
-        at = rows(j * block, block)
-        gathered_t[:, at] = gathered[at, :].T
-
-    for p in range(PARTS):
-        for dz in range(1, n_z):
-            z_gather(p, dz).wait_recv()
-            for d in range(1, n_y):
-                y_gather(p, dz, d).start()
 
     @pl.loop(1, n_z)
     def _(dz):
@@ -487,7 +516,12 @@
 
     for p in range(PARTS):
         for d in range(1, n_z):
-            z_gather(p, d).wait_send()
+            for way in range(2):
+
+                @pl.when(leaves(way, d))
+                def _(p=p, d=d, way=way):
+                    line_copy(p, way, d).wait_send()
+
         for d in range(1, n_y):
             for dz in range(n_z):
                 y_gather(p, dz, d).wait_send()
@@ -538,7 +572,7 @@
             dma((2, 2, PARTS, n_x)),
             dma((2, n_x, PARTS)),
             dma((2, n_x - 1, PARTS)),
-            dma((2, PARTS, n_z - 1)),
+            dma((2, 2, PARTS, n_z - 1)),
             dma((2, PARTS, n_z, n_y - 1)),
             pltpu.VMEM((total, CHUNK), bf16),
             pltpu.VMEM((items, n_z, tall, CHUNK), f32),

time: 161 us -> 156 us (0.969); the launches traced: 158 us -> 156 us
  Pallas kernels: 151 us -> 149 us
    pallas_call x1, Pallas kernels: 151 us -> 149 us  [step(): pl.pallas_call(functools.partial(step_kernel, n_x, n_y, n_z), out_shape=[...]
where the time goes in v3:
time: 156 us
  Pallas kernels  149 us (96%)
  local copies, waits for them, and re-layouts  6.16 us (4%)
    pallas_call x1, Pallas kernels, step(): pl.pallas_call(functools.partial(step_kernel, n_x, n_y, n_z), out_shape=[...  149 us
    unnamed x6, local copies, waits for them, and re-layouts  6.16 us

profile of v3, /device:TPU:0, one launch (start us, length us, event | category | flops | bytes accessed | tf_op | source)
XLA Modules:
  0.0 156.2 jit_solution(14883979648702943754)
XLA Ops:
  0.6 1.3 copy.8.neighbors
  2.0 149.4 %shard_map.76 = (f32[128,1024]{1,0:T(8,128)}, f32[1024,128]{1,0:T(8,128)}, f32[256,1024]{1,0:T(8,128)}) custom-call(bf16[256,1024]{1,0:T(8,128)(2,1)} %embeds.1, s32[1,256]{1,0:T(1,128)} %bitcast.1, s32[8,3]{1,0:T(8,128)} %copy.8.neighbors, bf16[1024,1024]{1,0:T(8,128)(2,1)} %w_first.1, bf16[1024,1024]{1,0:T(8,128)(2,1)} %w_second.1), custom_call_target="tpu_custom_call" | custom-call | tf_op jit(solution)/shard_map/pallas_call | solution.py:545
  151.4 0.0 copy-start
  151.4 2.0 %copy.12 = f32[128,1024]{1,0:T(8,128)} copy(f32[128,1024]{1,0:T(8,128)} %get-tuple-element.6) | data formatting | bytes 1048576
  153.4 1.9 %copy.13 = f32[1024,128]{1,0:T(8,128)} copy(f32[1024,128]{1,0:T(8,128)} %get-tuple-element.7) | data formatting | bytes 1048576
  155.3 0.0 copy-done
  155.3 1.0 copy.14
Async XLA Ops:
  151.4 3.9 %copy-start = (f32[256,1024]{1,0:T(8,128)S(1)}, f32[256,1024]{1,0:T(8,128)}, u32[]{:S(2)}) copy-start(f32[256,1024]{1,0:T(8,128)} %get-tuple-element.8) | copy-start | bytes 3145732
